TPU v7x, 32 devices: a whole 2x2x4 slice. The times are simulated.
32 devices in a mesh: node: 8 (over z, x), site: 4 (over y, core).
Axes of the slice: x: 2, y: 2, z: 4, core: 2. Of those that a mesh axis runs over, the one named last changes fastest.
Arguments:
- leaf_partials: float32 [512, 4, 4096], P('node', None, 'site'), may hold values from 0.05 to 1
- dag_edges: int32 [3, 1536, 3], P(None, 'node'), may hold values from 0 to 511, as said below
- weights: float32 [3, 1536], P(None, 'node'), may hold values from 0.25 to 4
- lengths: float32 [3, 1536], P(None, 'node'), may hold values from 0.02 to 2
- counts: int32 [4096], P('site'), may hold values from 1 to 9
- topo_nodes: int32 [32, 8], P('node'), may hold values from 0 to 511
Outputs:
- topology_loglik: float32 [32], P('node')
- edge_gradient: float32 [1536], P('node')
Inputs may be any that keep to these rules, and one draw needn't show every extreme that they name: `dag_edges`: in every level each subsplit is the child of exactly 3 edges, listed on the index of node that owns the child; subsplit n is owned by index n // 64. Column 1 is the parent in the next level, column 2 the rotation (0 or 1). Every parent has at least one edge of each rotation. Among the edges of one index of node, at most 32 have parents owned by any one index, and some index receives exactly 32 from every index.
All inputs are finite; a program needn't handle non-finite values.
Results may differ from a plain program's by a relative error of at most 0.0003.
Values sent between devices are 32-bit elements; how exact they have to be, the bound alone decides.
A program may use at most 192 MiB of HBM per device.

v0:
```python
import jax
import jax.numpy as jnp
from jax import lax
from jax.sharding import PartitionSpec as P


def transit(child_rows, branch):
    survival = jnp.exp(branch * (-4.0 / 3.0))[:, None, None]
    return survival * child_rows + (1.0 - survival) * 0.25 * jnp.sum(
        child_rows, axis=1, keepdims=True
    )


def on_device(leaf_partials, dag_edges, weights, lengths, counts, topo_nodes):
    node_dev, states, site_dev = leaf_partials.shape
    level_count, edge_dev = (dag_edges.shape[0], dag_edges.shape[1])
    owners = lax.axis_size("node")
    device = lax.axis_index("node")
    nodes_all = node_dev * owners
    sites_all = site_dev * lax.axis_size("site")
    scaled = counts.astype(jnp.float32) / sites_all
    incidence = lax.all_gather(topo_nodes, "node", axis=0, tiled=True)
    multiplicity = jax.ops.segment_sum(
        jnp.ones((incidence.size,), jnp.float32), incidence.reshape(-1), num_segments=nodes_all
    )
    capacity = 4 * node_dev // owners
    slots_all = owners * capacity
    current = leaf_partials
    for level_index in range(level_count):
        child_index = dag_edges[level_index, :, 0] - device * node_dev
        parents = dag_edges[level_index, :, 1]
        rotation = dag_edges[level_index, :, 2]
        message = transit(current[child_index], lengths[level_index])
        owner_dev = parents // node_dev
        one_hot = (owner_dev[:, None] == jnp.arange(owners)[None, :]).astype(jnp.int32)
        slot_rank = jnp.sum((jnp.cumsum(one_hot, axis=0) - one_hot) * one_hot, axis=1)
        slot_index = owner_dev * capacity + slot_rank
        pair_code = ((parents - owner_dev * node_dev) * 2 + rotation).astype(jnp.float32)
        buffer = jnp.zeros((slots_all, states, site_dev), jnp.float32).at[slot_index].set(message)
        code_buffer = jnp.full((slots_all,), -1.0, jnp.float32).at[slot_index].set(pair_code)
        weight_buffer = (
            jnp.zeros((slots_all,), jnp.float32).at[slot_index].set(weights[level_index])
        )
        received, received_codes, received_weights = (
            lax.all_to_all(
                buffer.reshape(owners, capacity, states, site_dev),
                "node",
                split_axis=0,
                concat_axis=0,
                tiled=True,
            ),
            lax.all_to_all(
                code_buffer.reshape(owners, capacity),
                "node",
                split_axis=0,
                concat_axis=0,
                tiled=True,
            ),
            lax.all_to_all(
                weight_buffer.reshape(owners, capacity),
                "node",
                split_axis=0,
                concat_axis=0,
                tiled=True,
            ),
        )
        flat_rows = received.reshape(slots_all, states * site_dev)
        selector = (
            received_codes.reshape(-1).astype(jnp.int32)[None, :]
            == jnp.arange(2 * node_dev)[:, None]
        ).astype(jnp.float32)
        summed = jnp.dot(
            selector * received_weights.reshape(-1)[None, :],
            flat_rows,
            precision=lax.Precision.HIGHEST,
            preferred_element_type=jnp.float32,
        )
        pair_sums = summed.reshape(node_dev, 2, states, site_dev)
        current = pair_sums[:, 0] * pair_sums[:, 1]
    denominator = 0.25 * jnp.sum(current, axis=1)
    node_part = jnp.sum(scaled[None, :] * jnp.log(denominator), axis=1)
    adjoint = pair_sums[:, ::-1] * (scaled[None, :] * 0.25 / denominator)[:, None, None, :]
    adjoint_slots = jnp.dot(
        selector.T,
        adjoint.reshape(2 * node_dev, states * site_dev),
        precision=lax.Precision.HIGHEST,
        preferred_element_type=jnp.float32,
    )
    grad_part = jnp.sum(flat_rows * adjoint_slots, axis=1)
    node_scores, slot_grads = lax.psum((node_part, grad_part), "site")
    own_mult = lax.dynamic_slice_in_dim(multiplicity, device * node_dev, node_dev)
    pair_mult = jnp.repeat(own_mult, 2)
    slot_mult = jnp.dot(
        selector.T, pair_mult, precision=lax.Precision.HIGHEST, preferred_element_type=jnp.float32
    )
    returned = lax.all_to_all(
        (slot_grads * slot_mult).reshape(owners, capacity),
        "node",
        split_axis=0,
        concat_axis=0,
        tiled=True,
    )
    edge_gradient = returned.reshape(-1)[slot_index]
    score_table = lax.all_gather(node_scores, "node", axis=0, tiled=True)
    topology_loglik = jnp.sum(score_table[topo_nodes], axis=1)
    return (topology_loglik, edge_gradient)


def solution(mesh):
    return jax.shard_map(
        on_device,
        mesh=mesh,
        in_specs=(
            P("node", None, "site"),
            P(None, "node", None),
            P(None, "node"),
            P(None, "node"),
            P("site"),
            P("node", None),
        ),
        out_specs=(P("node"), P("node")),
        check_vma=False,
    )
```

profile of v0, /device:TPU:0, one launch (start us, length us, event | category | flops | bytes accessed | tf_op | source)
XLA Modules:
  0.0 608.9 jit_solution(17417412113422156436)
XLA Ops:
  7.2 7.3 %all-to-all-start.4 = ((f32[8,1,32]{2,1,0:T(1,128)}), f32[8,1,32]{2,1,0:T(1,128)S(1)}, u32[]{:S(2)}, u32[]{:S(2)}) async-start(f32[8,1,32]{2,1,0:T(1,128)} %all_to_all.59), calls=%async_computation.4 | async-start | bytes 8192 | tf_op jit(solution)/shard_map/all_to_all | solution.py:52
  25.2 6.0 all-to-all-start.5
  38.0 26.2 %scatter_fusion = f32[256,4,1024]{2,1,0:T(4,128)} fusion(f32[256,4,1024]{2,1,0:T(4,128)} %broadcast.594.clone.1, s32[192]{0:T(256)S(1)} %bitcast.162, f32[192,4,1024]{2,1,0:T(4,128)} %multiply_add_fusion.2), kind=kCustom, calls=%fused_computation.11 | custom fusion | bytes 9437952 | tf_op jit(solution)/shard_map/scatter | solution.py:39
  64.2 6.5 %copy.22 = f32[8,32,4,1024]{3,1,2,0:T(8,128)} copy(f32[8,32,4,1024]{3,2,1,0:T(4,128)} %bitcast.134) | data formatting | bytes 8388608 | tf_op jit(solution)/shard_map/reshape | solution.py:46
  70.7 6.0 all-to-all-start.6
  82.0 86.8 %all-to-all-done.6 = f32[8,32,4,1024]{3,1,2,0:T(8,128)} async-done(((f32[8,32,4,1024]{3,1,2,0:T(8,128)}), f32[8,32,4,1024]{3,1,2,0:T(8,128)}, u32[]{:S(2)}, u32[]{:S(2)}) %all-to-all-start.6) | async-done | bytes 4194336 | tf_op jit(solution)/shard_map/all_to_all | solution.py:45
  177.4 5.7 copy.40
  183.1 5.8 copy.24
  188.9 6.6 %fusion.4 = f32[64,2,4,1024]{3,0,2,1:T(8,128)S(1)} fusion(f32[4,1024,256,1]{2,1,0,3:T(8,128)} %bitcast.137, f32[256]{0:T(256)S(1)} %mul.291, s32[256]{0:T(256)S(1)} %convert_element_type.69, s32[64,2]{0,1:T(2,128)S(1)} %multiply_add_fusion.3), kind=kOutput, calls=%fused_computation.32 | convolution fusion | flops 1610678272 | bytes 6294016 | tf_op jit(solution)/shard_map/dot_general | solution.py:72
  204.4 6.5 %all-to-all-start.3 = ((f32[8,1,32]{2,1,0:T(1,128)}), f32[8,1,32]{2,1,0:T(1,128)S(1)}, u32[]{:S(2)}, u32[]{:S(2)}) async-start(f32[8,1,32]{2,1,0:T(1,128)} %all_to_all.57), calls=%async_computation.3 | async-start | bytes 8192 | tf_op jit(solution)/shard_map/all_to_all | solution.py:59
  217.7 26.2 %scatter_fusion.1 = f32[256,4,1024]{2,1,0:T(4,128)} fusion(f32[256,4,1024]{2,1,0:T(4,128)} %broadcast.594.clone, s32[192]{0:T(256)S(1)} %bitcast.159, f32[192,4,1024]{2,1,0:T(4,128)} %multiply_add_fusion.1), kind=kCustom, calls=%fused_computation.12 | custom fusion | bytes 9437952 | tf_op jit(solution)/shard_map/scatter | solution.py:39
  243.9 6.5 %copy.27 = f32[8,32,4,1024]{3,1,2,0:T(8,128)} copy(f32[8,32,4,1024]{3,2,1,0:T(4,128)} %bitcast.135) | data formatting | bytes 8388608 | tf_op jit(solution)/shard_map/reshape | solution.py:46
  250.4 6.0 all-to-all-start.7
  261.0 87.7 %all-to-all-done.7 = f32[8,32,4,1024]{3,1,2,0:T(8,128)} async-done(((f32[8,32,4,1024]{3,1,2,0:T(8,128)}), f32[8,32,4,1024]{3,1,2,0:T(8,128)}, u32[]{:S(2)}, u32[]{:S(2)}) %all-to-all-start.7) | async-done | bytes 4194336 | tf_op jit(solution)/shard_map/all_to_all | solution.py:45
  357.5 5.7 copy.41
  363.2 5.8 copy.29
  369.0 6.6 %fusion.6 = f32[64,2,4,1024]{3,0,2,1:T(8,128)S(1)} fusion(f32[4,1024,256,1]{2,1,0,3:T(8,128)} %bitcast.138, f32[256]{0:T(256)S(1)} %mul.282, s32[256]{0:T(256)S(1)} %convert_element_type.65, s32[64,2]{0,1:T(2,128)S(1)} %multiply_add_fusion.3), kind=kOutput, calls=%fused_computation.34 | convolution fusion | flops 1610678272 | bytes 6294016 | tf_op jit(solution)/shard_map/dot_general | solution.py:72
  384.4 6.0 all-to-all-start.1
  397.2 26.1 %scatter_fusion.2 = f32[256,4,1024]{2,1,0:T(4,128)} fusion(f32[256,4,1024]{2,1,0:T(4,128)} %broadcast.594, s32[192]{0:T(256)S(1)} %bitcast.148, f32[192,4,1024]{2,1,0:T(4,128)} %multiply_add_fusion), kind=kCustom, calls=%fused_computation.13 | custom fusion | bytes 9437952 | tf_op jit(solution)/shard_map/scatter | solution.py:39
  423.4 6.2 %all-to-all-start.8 = ((f32[8,32,4,1024]{3,2,1,0:T(4,128)}), f32[8,32,4,1024]{3,2,1,0:T(4,128)}, u32[]{:S(2)}, u32[]{:S(2)}) async-start(f32[8,32,4,1024]{3,2,1,0:T(4,128)} %bitcast.136), calls=%async_computation.8 | async-start | bytes 8388608 | tf_op jit(solution)/shard_map/all_to_all | solution.py:45
  429.6 110.7 %all-gather = s32[8,4,8]{2,1,0:T(4,128)S(1)} all-gather(s32[1,4,8]{2,1,0:T(4,128)S(1)} %bitcast.156), channel_id=1, replica_groups=mesh['node'=8,'site'=4] {'node'}, dimensions={0}, use_global_device_ids=true | all-gather | bytes 1152 | tf_op jit(solution)/shard_map/all_gather | solution.py:22
  544.4 8.0 %copy.42 = f32[32,8,4,1024]{3,1,2,0:T(8,128)} copy(f32[32,8,4,1024]{3,2,1,0:T(4,128)} %bitcast.75) | data formatting | bytes 8388608
  558.0 6.6 %fusion.8 = f32[64,2,4,1024]{3,0,2,1:T(8,128)S(1)} fusion(f32[4,1024,256,1]{2,1,0,3:T(8,128)} %bitcast.139, f32[256]{0:T(256)S(1)} %mul.273, s32[64,2]{0,1:T(2,128)S(1)} %multiply_add_fusion.3, s32[256]{0:T(256)S(1)} %convert_element_type.61), kind=kOutput, calls=%fused_computation.36 | convolution fusion | flops 1610678272 | bytes 6294016 | tf_op jit(solution)/shard_map/dot_general | solution.py:72
  582.4 21.7 %all-reduce.3 = f32[512]{0:T(512)S(1)} all-reduce(f32[512]{0:T(512)S(1)} %dynamic-update-slice), channel_id=1, replica_groups=mesh['node'=8,'site'=4] {'node'}, use_global_device_ids=true, to_apply=%add.3 | all-reduce | flops 512 | bytes 4096
  (140 shorter events, 113.5 us)
Async XLA Ops:
  0.6 14.7 %copy-start = (f32[64,4,1024]{2,1,0:T(4,128)S(1)}, f32[64,4,1024]{2,1,0:T(4,128)}, u32[]{:S(2)}) copy-start(f32[64,4,1024]{2,1,0:T(4,128)} %param.6) | copy-start | bytes 3145732
  7.2 18.0 %all-to-all-start.4 = ((f32[8,1,32]{2,1,0:T(1,128)}), f32[8,1,32]{2,1,0:T(1,128)S(1)}, u32[]{:S(2)}, u32[]{:S(2)}) async-start(f32[8,1,32]{2,1,0:T(1,128)} %all_to_all.59), calls=%async_computation.4 | async-start | bytes 8192 | tf_op jit(solution)/shard_map/all_to_all | solution.py:52
  19.4 3.9 copy-start.5
  25.2 45.5 %all-to-all-start.5 = ((f32[8,1,32]{2,1,0:T(1,128)}), f32[8,1,32]{2,1,0:T(1,128)S(1)}, u32[]{:S(2)}, u32[]{:S(2)}) async-start(f32[8,1,32]{2,1,0:T(1,128)} %all_to_all.61), calls=%async_computation.5 | async-start | bytes 8192 | tf_op jit(solution)/shard_map/all_to_all | solution.py:59
  70.7 98.1 %all-to-all-start.6 = ((f32[8,32,4,1024]{3,1,2,0:T(8,128)}), f32[8,32,4,1024]{3,1,2,0:T(8,128)}, u32[]{:S(2)}, u32[]{:S(2)}) async-start(f32[8,32,4,1024]{3,1,2,0:T(8,128)} %copy.22), calls=%async_computation.6 | async-start | bytes 8388608 | tf_op jit(solution)/shard_map/all_to_all | solution.py:45
  168.8 35.5 %all-to-all-start.2 = ((f32[8,1,32]{2,1,0:T(1,128)}), f32[8,1,32]{2,1,0:T(1,128)S(1)}, u32[]{:S(2)}, u32[]{:S(2)}) async-start(f32[8,1,32]{2,1,0:T(1,128)} %all_to_all.55), calls=%async_computation.2 | async-start | bytes 8192 | tf_op jit(solution)/shard_map/all_to_all | solution.py:52
  204.4 46.0 %all-to-all-start.3 = ((f32[8,1,32]{2,1,0:T(1,128)}), f32[8,1,32]{2,1,0:T(1,128)S(1)}, u32[]{:S(2)}, u32[]{:S(2)}) async-start(f32[8,1,32]{2,1,0:T(1,128)} %all_to_all.57), calls=%async_computation.3 | async-start | bytes 8192 | tf_op jit(solution)/shard_map/all_to_all | solution.py:59
  250.4 98.3 %all-to-all-start.7 = ((f32[8,32,4,1024]{3,1,2,0:T(8,128)}), f32[8,32,4,1024]{3,1,2,0:T(8,128)}, u32[]{:S(2)}, u32[]{:S(2)}) async-start(f32[8,32,4,1024]{3,1,2,0:T(8,128)} %copy.27), calls=%async_computation.7 | async-start | bytes 8388608 | tf_op jit(solution)/shard_map/all_to_all | solution.py:45
  348.7 35.7 %all-to-all-start = ((f32[8,1,32]{2,1,0:T(1,128)}), f32[8,1,32]{2,1,0:T(1,128)S(1)}, u32[]{:S(2)}, u32[]{:S(2)}) async-start(f32[8,1,32]{2,1,0:T(1,128)} %all_to_all.51), calls=%async_computation | async-start | bytes 8192 | tf_op jit(solution)/shard_map/all_to_all | solution.py:52
  384.4 39.0 %all-to-all-start.1 = ((f32[8,1,32]{2,1,0:T(1,128)}), f32[8,1,32]{2,1,0:T(1,128)S(1)}, u32[]{:S(2)}, u32[]{:S(2)}) async-start(f32[8,1,32]{2,1,0:T(1,128)} %all_to_all.53), calls=%async_computation.1 | async-start | bytes 8192 | tf_op jit(solution)/shard_map/all_to_all | solution.py:59
  423.4 6.2 %copy-start.3 = (s32[4,8]{1,0:T(4,128)S(1)}, s32[4,8]{1,0:T(4,128)}, u32[]{:S(2)}) copy-start(s32[4,8]{1,0:T(4,128)} %param.11) | copy-start | bytes 388
  423.4 120.0 %copy-start.4 = (s32[1024]{0:T(1024)S(1)}, s32[1024]{0:T(1024)}, u32[]{:S(2)}) copy-start(s32[1024]{0:T(1024)} %param.10) | copy-start | bytes 12292
  423.4 121.0 %all-to-all-start.8 = ((f32[8,32,4,1024]{3,2,1,0:T(4,128)}), f32[8,32,4,1024]{3,2,1,0:T(4,128)}, u32[]{:S(2)}, u32[]{:S(2)}) async-start(f32[8,32,4,1024]{3,2,1,0:T(4,128)} %bitcast.136), calls=%async_computation.8 | async-start | bytes 8388608 | tf_op jit(solution)/shard_map/all_to_all | solution.py:45
  566.6 2.2 copy-start.2
  568.8 12.1 %copy-start.6 = (u32[32]{0:T(128)S(1)}, u32[32]{0:T(128)}, u32[]{:S(2)}) copy-start(u32[32]{0:T(128)} %constant.96) | copy-start | bytes 388
  568.8 39.7 %copy-start.1 = (f32[64,4,1024]{2,1,0:T(4,128)S(1)}, f32[64,4,1024]{2,1,0:T(4,128)}, u32[]{:S(2)}) copy-start(f32[64,4,1024]{2,1,0:T(4,128)} %param.6) | copy-start | bytes 3145732
  577.5 28.0 %all-to-all-start.9 = ((f32[8,1,32]{2,1,0:T(1,128)}), f32[8,1,32]{2,1,0:T(1,128)S(1)}, u32[]{:S(2)}, u32[]{:S(2)}) async-start(f32[8,1,32]{2,1,0:T(1,128)} %all_to_all.66), calls=%async_computation.9 | async-start | bytes 8192 | tf_op jit(solution)/shard_map/all_to_all | solution.py:96
where the time goes:
time: 620 us; the launch traced here: 609 us
  local copies, waits for them, and re-layouts  183 us (30%)
  waiting for transfers between devices  175 us (28%)
  blocking collectives  138 us (22%)
  starting transfers between devices  54.7 us (9%)
  other arithmetic  33.9 us (5%)
  matrix products  22.3 us (4%)
    all_to_all x3, waiting for transfers between devices, on_device(): lax.all_to_all(buffer.reshape(owners, capacity, states, site_dev), 'node'...  175 us
    all_gather x1, blocking collectives, on_device(): incidence = lax.all_gather(topo_nodes, 'node', axis=0, tiled=True)  111 us
    scatter x3, local copies, waits for them, and re-layouts, on_device(): jnp.zeros((slots_all, states, site_dev), jnp.float32).at[slot_index]  78.5 us
    unnamed x21, local copies, waits for them, and re-layouts  22.4 us
    unnamed x1, blocking collectives  21.7 us
    dot_general x3, matrix products, on_device(): jnp.dot(selector * received_weights.reshape(-1)[None, :], flat_rows, prec...  19.7 us
    all_to_all x3, starting transfers between devices, on_device(): lax.all_to_all(weight_buffer.reshape(owners, capacity), 'node', split_axi...  18.5 us
    all_to_all x3, starting transfers between devices, on_device(): lax.all_to_all(buffer.reshape(owners, capacity, states, site_dev), 'node'...  18.1 us
  transfers between devices with their start and end apart: 10, of which 2 were waited for; matrix products, arithmetic and copies ran while one was open for 33% of the time, Pallas kernels for 0%

commit v1 on v0

--- a/solution.py
+++ b/solution.py
@@ -1,6 +1,10 @@
+import functools
+
 import jax
 import jax.numpy as jnp
 from jax import lax
+from jax.experimental import pallas as pl
+from jax.experimental.pallas import tpu as pltpu
 from jax.sharding import PartitionSpec as P
 
 
@@ -106,9 +110,407 @@
     return (topology_loglik, edge_gradient)
 
 
+MESH = pl.DeviceIdType.MESH
+F32 = jnp.float32
+BF16 = jnp.bfloat16
+ROW = 256
+SIDE = 128
+
+
+def halves(x):
+    hi = x.astype(BF16)
+    return hi, (x - hi.astype(F32)).astype(BF16)
+
+
+def mm(a, b):
+    return jnp.dot(a, b, preferred_element_type=F32)
+
+
+def mm_nt(a, b):
+    return lax.dot_general(a, b, (((1,), (1,)), ((), ())), preferred_element_type=F32)
+
+
+def kernel(
+    dims,
+    leaf,
+    meta,
+    scaled,
+    out,
+    inbox,
+    tables,
+    m1h,
+    m1l,
+    m2h,
+    m2l,
+    picks,
+    gmat,
+    chi,
+    clo,
+    shi,
+    slo,
+    cur,
+    pair,
+    ahi,
+    alo,
+    shadj_hi,
+    shadj_lo,
+    dst,
+    mult,
+    send1,
+    recv1,
+    send2,
+    recv2,
+    leaf_send,
+    leaf_recv,
+    meta_send,
+    meta_recv,
+    own_sem,
+    r1_send,
+    r1_recv,
+    r2_send,
+    r2_recv,
+):
+    owners, site_ways, node_dev, states, levels, topo_here = dims
+    nodes = owners * node_dev
+    me = lax.axis_index("node")
+    my_site = lax.axis_index("site")
+
+    barrier = pltpu.get_barrier_semaphore()
+    for i in range(1, owners):
+        pl.semaphore_signal(
+            barrier, inc=1, device_id={"node": lax.rem(me + i, owners)}, device_id_type=MESH
+        )
+    for i in range(1, site_ways):
+        pl.semaphore_signal(
+            barrier, inc=1, device_id={"site": lax.rem(my_site + i, site_ways)}, device_id_type=MESH
+        )
+    pl.semaphore_wait(barrier, owners - 1 + site_ways - 1)
+
+    meta_copies, leaf_copies = [], []
+    for i in range(1, owners):
+        copy = pltpu.make_async_remote_copy(
+            src_ref=meta,
+            dst_ref=tables.at[i],
+            send_sem=meta_send.at[i],
+            recv_sem=meta_recv.at[i],
+            device_id={"node": lax.rem(me + i, owners)},
+            device_id_type=MESH,
+        )
+        copy.start()
+        meta_copies.append(copy)
+    own_meta = pltpu.make_async_copy(meta, tables.at[0], own_sem.at[0])
+    own_meta.start()
+    for i in range(1, owners):
+        target = lax.rem(me + i, owners)
+        copy = pltpu.make_async_remote_copy(
+            src_ref=leaf.at[:, :, pl.ds(pl.multiple_of(target * SIDE, SIDE), SIDE)],
+            dst_ref=inbox.at[i],
+            send_sem=leaf_send.at[i],
+            recv_sem=leaf_recv.at[i],
+            device_id={"node": target},
+            device_id_type=MESH,
+        )
+        copy.start()
+        leaf_copies.append(copy)
+    own_leaf = pltpu.make_async_copy(
+        leaf.at[:, :, pl.ds(pl.multiple_of(me * SIDE, SIDE), SIDE)], inbox.at[0], own_sem.at[1]
+    )
+    own_leaf.start()
+
+    own_meta.wait()
+    for copy in meta_copies:
+        copy.wait_recv()
+
+    def absolute(first, rows):
+        row = lax.broadcasted_iota(jnp.int32, (rows, SIDE), 0) + first
+        node = lax.rem(row, nodes)
+        owner = lax.rem(me - node // node_dev + owners, owners)
+        code = (row // nodes) * nodes + owner * node_dev + lax.rem(node, node_dev)
+        return code.astype(F32)[:, :1]
+
+    lane = lax.broadcasted_iota(jnp.int32, (1, SIDE), 1)
+    topo_lane = (lane >= SIDE // 2) & (lane < SIDE // 2 + topo_here)
+    child_iota = lax.broadcasted_iota(jnp.int32, (2 * node_dev, ROW), 0).astype(F32)
+
+    chunk = 256
+
+    def build(step, carry):
+        level = step // (owners // 2)
+        duo = lax.rem(step, owners // 2)
+        codes = []
+        for a in range(2):
+            child = tables[2 * duo + a, level, 0:1, :]
+            codes.append(tables[2 * duo + a, level, 1:2, :])
+            weight = tables[2 * duo + a, level, 2:3, :]
+            q = tables[2 * duo + a, level, 3:4, :]
+            hot = child_iota == child + float(a * node_dev)
+            g1h, g1l = halves(jnp.where(hot, weight * q, 0.0))
+            g2h, g2l = halves(jnp.where(hot, weight * (1.0 - q) * 0.25, 0.0))
+            columns = slice(a * ROW, (a + 1) * ROW)
+            for n, piece in enumerate((g1h, g1l, g2h, g2l)):
+                gmat[n * SIDE : (n + 1) * SIDE, columns] = piece
+        code = jnp.concatenate(codes, axis=1)
+        where_to = pl.ds(pl.multiple_of(duo * SIDE, SIDE), SIDE)
+        for first in range(0, 2 * nodes, chunk):
+            pick = jnp.where(absolute(first, chunk) == code, 1.0, 0.0).astype(BF16)
+            rows = slice(first, first + chunk)
+
+            @pl.when(level == levels - 1)
+            def _():
+                picks[duo, rows, :] = pick
+
+            found = mm_nt(pick, gmat[...])
+            hi, lo = halves(found[:, :SIDE] + found[:, SIDE : 2 * SIDE])
+            m1h[level, rows, where_to] = hi
+            m1l[level, rows, where_to] = lo
+            hi, lo = halves(found[:, 2 * SIDE : 3 * SIDE] + found[:, 3 * SIDE :])
+            m2h[level, rows, where_to] = hi
+            m2l[level, rows, where_to] = lo
+        return carry
+
+    lax.fori_loop(0, levels * (owners // 2), build, 0)
+
+    node_abs = absolute(0, nodes)
+    times = jnp.zeros((nodes, SIDE), F32)
+    for i in range(owners):
+        wanted = jnp.where(topo_lane, tables[i, levels - 1, 0:1, SIDE:], -1.0)
+        times += jnp.where(node_abs == wanted, 1.0, 0.0)
+    mult[...] = jnp.broadcast_to(jnp.sum(times, axis=1, keepdims=True), (nodes, SIDE))
+
+    own_leaf.wait()
+    for i in range(owners):
+        if i:
+            leaf_copies[i - 1].wait_recv()
+        block = inbox[i]
+        rows = slice(i * node_dev, (i + 1) * node_dev)
+        for k in range(states):
+            cur[rows, k * SIDE : (k + 1) * SIDE] = block[:, k, :]
+
+    def split(first, carry):
+        rows = pl.ds(pl.multiple_of(first * SIDE, SIDE), SIDE)
+        x = cur[rows, :]
+        chi[rows, :], clo[rows, :] = halves(x)
+        total = x[:, :SIDE]
+        for k in range(1, states):
+            total = total + x[:, k * SIDE : (k + 1) * SIDE]
+        shi[rows, :], slo[rows, :] = halves(total)
+        return carry
+
+    for level in range(levels):
+        lax.fori_loop(0, nodes // SIDE, split, 0)
+
+        def advance(step, carry, level=level):
+            rows = pl.ds(pl.multiple_of(step * SIDE, SIDE), SIDE)
+            made = []
+            for r in range(2):
+                source = pl.ds(pl.multiple_of(r * nodes + step * SIDE, SIDE), SIDE)
+                ah, al = m1h[level, source, :], m1l[level, source, :]
+                bh, bl = m2h[level, source, :], m2l[level, source, :]
+                flat = mm(bh, shi[...]) + mm(bh, slo[...]) + mm(bl, shi[...])
+                full = mm(ah, chi[...]) + mm(ah, clo[...]) + mm(al, chi[...])
+                made.append(full + jnp.concatenate([flat] * states, axis=1))
+                if level == levels - 1:
+                    pair[source, :] = made[r]
+            cur[rows, :] = made[0] * made[1]
+            return carry
+
+        lax.fori_loop(0, nodes // SIDE, advance, 0)
+
+    site_row = lax.broadcasted_iota(jnp.int32, scaled.shape, 0)
+    count = jnp.sum(jnp.where(site_row == me, scaled[...], 0.0), axis=0, keepdims=True)
+    picked = [jnp.zeros((1, SIDE), F32)] * owners
+    for first in range(0, nodes, SIDE):
+        rows = slice(first, first + SIDE)
+        x = cur[rows, :]
+        total = x[:, :SIDE]
+        for k in range(1, states):
+            total = total + x[:, k * SIDE : (k + 1) * SIDE]
+        lik = 0.25 * total
+        score = jnp.sum(count * jnp.log(lik), axis=1, keepdims=True)
+        here = absolute(first, SIDE)
+        for i in range(owners):
+            wanted = jnp.where(topo_lane, tables[i, levels - 1, 0:1, SIDE:], -1.0)
+            picked[i] = picked[i] + jnp.sum(
+                jnp.where(here == wanted, score, 0.0), axis=0, keepdims=True
+            )
+        factor = count * 0.25 / lik * mult[rows, :]
+        wide = jnp.concatenate([factor] * states, axis=1)
+        for r in range(2):
+            adj = pair[(1 - r) * nodes + first : (1 - r) * nodes + first + SIDE, :] * wide
+            to = slice(r * nodes + first, r * nodes + first + SIDE)
+            ahi[to, :], alo[to, :] = halves(adj)
+            flat = adj[:, :SIDE]
+            for k in range(1, states):
+                flat = flat + adj[:, k * SIDE : (k + 1) * SIDE]
+            shadj_hi[to, :], shadj_lo[to, :] = halves(flat)
+
+    def products(step, carry):
+        cols = pl.ds(pl.multiple_of(step * ROW, ROW), ROW)
+        ah, al = ahi[cols, :], alo[cols, :]
+        sh, sl = shadj_hi[cols, :], shadj_lo[cols, :]
+        d1 = mm_nt(chi[...], ah) + mm_nt(chi[...], al) + mm_nt(clo[...], ah)
+        d2 = mm_nt(shi[...], sh) + mm_nt(shi[...], sl) + mm_nt(slo[...], sh)
+        d1h, d1l = halves(d1)
+        d2h, d2l = halves(d2)
+        for i in range(owners):
+            rows = slice(i * node_dev, (i + 1) * node_dev)
+            for n, piece in enumerate((d1h, d1l, d2h, d2l)):
+                dst[i, n * node_dev : (n + 1) * node_dev, cols] = piece[rows, :]
+        return carry
+
+    lax.fori_loop(0, 2 * nodes // ROW, products, 0)
+
+    edge_iota = lax.broadcasted_iota(jnp.int32, (node_dev, ROW), 0).astype(F32)
+    last = levels - 1
+    for i in range(owners):
+        found = mm(dst[i], picks[i // 2, :, (i % 2) * ROW : (i % 2 + 1) * ROW])
+        hot = edge_iota == tables[i, last, 0:1, :]
+        d1 = found[:node_dev] + found[node_dev : 2 * node_dev]
+        d2 = found[2 * node_dev : 3 * node_dev] + found[3 * node_dev :]
+        q = tables[i, last, 3:4, :]
+        mixed = jnp.where(hot, q * d1 + (1.0 - q) * 0.25 * d2, 0.0)
+        grads = jnp.sum(mixed, axis=0, keepdims=True)
+        grads = grads + jnp.concatenate([jnp.zeros((1, SIDE), F32), picked[i]], axis=1)
+        send1[i] = jnp.broadcast_to(grads, (8, ROW))
+
+    first_copies = []
+    for i in range(1, owners):
+        copy = pltpu.make_async_remote_copy(
+            src_ref=send1.at[i],
+            dst_ref=recv1.at[i],
+            send_sem=r1_send.at[i],
+            recv_sem=r1_recv.at[i],
+            device_id={"node": lax.rem(me - i + owners, owners)},
+            device_id_type=MESH,
+        )
+        copy.start()
+        first_copies.append(copy)
+    total = send1[0]
+    for i in range(1, owners):
+        first_copies[i - 1].wait_recv()
+        total = total + recv1[i]
+    send2[...] = total
+    recv2[my_site] = total
+    second_copies = []
+    for i in range(1, site_ways):
+        copy = pltpu.make_async_remote_copy(
+            src_ref=send2,
+            dst_ref=recv2.at[my_site],
+            send_sem=r2_send.at[i],
+            recv_sem=r2_recv.at[i],
+            device_id={"site": lax.rem(my_site + i, site_ways)},
+            device_id_type=MESH,
+        )
+        copy.start()
+        second_copies.append(copy)
+    for copy in second_copies:
+        copy.wait_recv()
+    total = recv2[0]
+    for i in range(1, site_ways):
+        total = total + recv2[i]
+    out[...] = total
+    for copy in meta_copies + leaf_copies + first_copies + second_copies:
+        copy.wait_send()
+
+
+def by_sites(leaf_partials, dag_edges, weights, lengths, counts, topo_nodes):
+    node_dev, states, site_dev = leaf_partials.shape
+    levels, edge_dev, _ = dag_edges.shape
+    owners, site_ways = lax.axis_size("node"), lax.axis_size("site")
+    nodes = owners * node_dev
+    topo_here = topo_nodes.size
+    edges = jnp.transpose(dag_edges, (2, 0, 1))
+    child = edges[0] - lax.axis_index("node") * node_dev
+    code = edges[2] * nodes + edges[1]
+    tail = ROW - edge_dev
+    extra = jnp.pad(topo_nodes.reshape(-1), (0, tail - topo_here))
+    child = jnp.concatenate([child, jnp.broadcast_to(extra, (levels, tail))], axis=1)
+    pad = ((0, 0), (0, tail))
+    meta = jnp.stack(
+        [
+            child.astype(F32),
+            jnp.pad(code, pad, constant_values=-1).astype(F32),
+            jnp.pad(weights, pad),
+            jnp.pad(jnp.exp(lengths * (-4.0 / 3.0)), pad),
+        ],
+        axis=1,
+    )
+    scaled = (counts.astype(F32) / (site_dev * site_ways)).reshape(owners, SIDE)
+    wide = states * SIDE
+    out = pl.pallas_call(
+        functools.partial(
+            kernel, (owners, site_ways, node_dev, states, levels, topo_here)
+        ),
+        out_shape=jax.ShapeDtypeStruct((8, ROW), F32),
+        in_specs=[
+            pl.BlockSpec(memory_space=pl.ANY),
+            pl.BlockSpec(memory_space=pltpu.VMEM),
+            pl.BlockSpec(memory_space=pltpu.VMEM),
+        ],
+        out_specs=pl.BlockSpec(memory_space=pltpu.VMEM),
+        scratch_shapes=[
+            pltpu.VMEM((owners, node_dev, states, SIDE), F32),
+            pltpu.VMEM((owners, levels, 4, ROW), F32),
+            pltpu.VMEM((levels, 2 * nodes, nodes), BF16),
+            pltpu.VMEM((levels, 2 * nodes, nodes), BF16),
+            pltpu.VMEM((levels, 2 * nodes, nodes), BF16),
+            pltpu.VMEM((levels, 2 * nodes, nodes), BF16),
+            pltpu.VMEM((owners // 2, 2 * nodes, 2 * ROW), BF16),
+            pltpu.VMEM((4 * SIDE, 2 * ROW), BF16),
+            pltpu.VMEM((nodes, wide), BF16),
+            pltpu.VMEM((nodes, wide), BF16),
+            pltpu.VMEM((nodes, SIDE), BF16),
+            pltpu.VMEM((nodes, SIDE), BF16),
+            pltpu.VMEM((nodes, wide), F32),
+            pltpu.VMEM((2 * nodes, wide), F32),
+            pltpu.VMEM((2 * nodes, wide), BF16),
+            pltpu.VMEM((2 * nodes, wide), BF16),
+            pltpu.VMEM((2 * nodes, SIDE), BF16),
+            pltpu.VMEM((2 * nodes, SIDE), BF16),
+            pltpu.VMEM((owners, 4 * node_dev, 2 * nodes), BF16),
+            pltpu.VMEM((nodes, SIDE), F32),
+            pltpu.VMEM((owners, 8, ROW), F32),
+            pltpu.VMEM((owners, 8, ROW), F32),
+            pltpu.VMEM((8, ROW), F32),
+            pltpu.VMEM((site_ways, 8, ROW), F32),
+            pltpu.SemaphoreType.DMA((owners,)),
+            pltpu.SemaphoreType.DMA((owners,)),
+            pltpu.SemaphoreType.DMA((owners,)),
+            pltpu.SemaphoreType.DMA((owners,)),
+            pltpu.SemaphoreType.DMA((2,)),
+            pltpu.SemaphoreType.DMA((owners,)),
+            pltpu.SemaphoreType.DMA((owners,)),
+            pltpu.SemaphoreType.DMA((site_ways,)),
+            pltpu.SemaphoreType.DMA((site_ways,)),
+        ],
+        compiler_params=pltpu.CompilerParams(
+            collective_id=0, has_side_effects=True, vmem_limit_bytes=50 * 2**20
+        ),
+    )(leaf_partials, meta, scaled)
+    loglik = jnp.sum(
+        out[0, edge_dev : edge_dev + topo_here].reshape(topo_nodes.shape), axis=1
+    )
+    return loglik, out[0, :edge_dev]
+
+
+def either(leaf_partials, dag_edges, weights, lengths, counts, topo_nodes):
+    node_dev, states, site_dev = leaf_partials.shape
+    owners = lax.axis_size("node")
+    fits = (
+        site_dev == owners * SIDE
+        and 2 * node_dev == SIDE
+        and owners % 2 == 0
+        and owners <= 8
+        and dag_edges.shape[1] == ROW * 3 // 4
+        and topo_nodes.size <= ROW // 4
+    )
+    form = by_sites if fits else on_device
+    return form(leaf_partials, dag_edges, weights, lengths, counts, topo_nodes)
+
+
 def solution(mesh):
     return jax.shard_map(
-        on_device,
+        either,
         mesh=mesh,
         in_specs=(
             P("node", None, "site"),

time: 620 us -> 73.7 us (0.12); the launches traced: 609 us -> 73.4 us
  local copies, waits for them, and re-layouts: 183 us -> 5.53 us
  waiting for transfers between devices: 175 us -> 0 us
  blocking collectives: 138 us -> 0 us
  Pallas kernels: 0 us -> 66.5 us
  starting transfers between devices: 54.7 us -> 0 us
  other arithmetic: 33.9 us -> 0.68 us
  matrix products: 22.3 us -> 0 us
    all_to_all x10 -> x0, waiting for transfers between devices: 175 us -> none  [the longest x3 175 us: on_device(): lax.all_to_all(buffer.reshape(owners, capacity, states, site_dev), 'node'...]
    all_gather x1 -> x0, blocking collectives: 111 us -> none  [on_device(): incidence = lax.all_gather(topo_nodes, 'node', axis=0, tiled=True)]
    scatter x9 -> x0, local copies, waits for them, and re-layouts: 85.9 us -> none  [the longest x3 78.5 us: on_device(): jnp.zeros((slots_all, states, site_dev), jnp.float32).at[slot_index]]
    pallas_call x0 -> x1, Pallas kernels: none -> 66.5 us  [by_sites(): pl.pallas_call(functools.partial(kernel, (owners, site_ways, node_dev, st...]
    all_to_all x10 -> x0, starting transfers between devices: 54.7 us -> none  [the longest x3 18.5 us: on_device(): lax.all_to_all(weight_buffer.reshape(owners, capacity), 'node', split_axi...]
    dot_general x5 -> x0, matrix products: 22.3 us -> none  [the longest x3 19.7 us: on_device(): jnp.dot(selector * received_weights.reshape(-1)[None, :], flat_rows, prec...]
    unnamed x1 -> x0, blocking collectives: 21.7 us -> none
    unnamed x21 -> x11, local copies, waits for them, and re-layouts: 22.4 us -> 4.61 us
  transfers between devices with their start and end apart: 10 -> 0, of which waited for: 2 -> 0; matrix products, arithmetic and copies ran while one was open for 33% -> 0% of each run, Pallas kernels for 0% -> 0%
where the time goes in v1:
time: 73.7 us; the launch traced here: 73.4 us
  Pallas kernels  66.5 us (90%)
  local copies, waits for them, and re-layouts  5.53 us (8%)
    pallas_call x1, Pallas kernels, by_sites(): pl.pallas_call(functools.partial(kernel, (owners, site_ways, node_dev, st...  66.5 us
    unnamed x11, local copies, waits for them, and re-layouts  4.61 us

profile of v1, /device:TPU:0, one launch (start us, length us, event | category | flops | bytes accessed | tf_op | source)
XLA Modules:
  0.0 73.4 jit_solution(13640534111723880770)
XLA Ops:
  0.6 0.7 copy.11
  1.3 0.0 copy-start.4
  1.4 0.7 copy-done.4
  2.0 0.1 reshape.47
  2.1 0.1 pad.25
  2.2 0.0 copy-start.1
  2.2 0.7 copy-done.1
  2.9 0.0 copy-start.2
  2.9 0.7 copy-done.2
  3.6 0.0 copy-start.3
  3.7 0.7 copy-done.3
  4.3 0.0 copy-start
  4.3 1.2 %copy-done = f32[64,4,1024]{2,1,0:T(4,128)S(1)} copy-done((f32[64,4,1024]{2,1,0:T(4,128)S(1)}, f32[64,4,1024]{2,1,0:T(4,128)}, u32[]{:S(2)}) %copy-start) | copy-done | bytes 1048600
  5.5 66.5 %shard_map.77 = f32[8,256]{1,0:T(8,128)S(1)} custom-call(f32[64,4,1024]{2,1,0:T(4,128)S(1)} %copy-done, f32[3,4,256]{2,1,0:T(4,128)S(1)} %pad_maximum_fusion.meta, f32[8,128]{1,0:T(8,128)S(1)} %multiply_bitcast_fusion.scaled), custom_call_target="tpu_custom_call" | custom-call | tf_op jit(solution)/shard_map/pallas_call | solution.py:440
  72.0 0.1 slice_reduce_fusion
  72.1 0.1 reshape_squeeze.3
  72.2 0.6 reduce_sum.9
  72.8 0.6 slice.19
  (12 shorter events, 0.1 us)
Async XLA Ops:
  1.3 0.7 copy-start.4
  2.2 0.7 copy-start.1
  2.9 0.7 copy-start.2
  3.6 0.7 copy-start.3
  4.3 1.2 %copy-start = (f32[64,4,1024]{2,1,0:T(4,128)S(1)}, f32[64,4,1024]{2,1,0:T(4,128)}, u32[]{:S(2)}) copy-start(f32[64,4,1024]{2,1,0:T(4,128)} %leaf.1) | copy-start | bytes 3145732

commit v2 on v1

--- a/solution.py
+++ b/solution.py
@@ -133,9 +133,19 @@
 def kernel(
     dims,
     leaf,
+    edges_hbm,
+    weights_hbm,
+    lengths_hbm,
+    counts_hbm,
+    topo_hbm,
+    loglik_out,
+    grad_out,
+    edges,
+    weights,
+    lengths,
+    counts,
+    topo,
     meta,
-    scaled,
-    out,
     inbox,
     tables,
     m1h,
@@ -144,17 +154,16 @@
     m2l,
     picks,
     gmat,
-    chi,
-    clo,
-    shi,
-    slo,
-    cur,
+    ch,
+    cl,
+    sums,
     pair,
+    lik_sum,
     ahi,
     alo,
-    shadj_hi,
-    shadj_lo,
+    adj_sums,
     dst,
+    numbers,
     mult,
     send1,
     recv1,
@@ -170,10 +179,30 @@
     r2_send,
     r2_recv,
 ):
-    owners, site_ways, node_dev, states, levels, topo_here = dims
+    owners, site_ways, node_dev, states, levels, topo_shape, sites_all = dims
     nodes = owners * node_dev
+    edge_dev = edges.shape[2]
+    topo_here = topo_shape[0] * topo_shape[1]
     me = lax.axis_index("node")
     my_site = lax.axis_index("site")
+
+    small = []
+    for n, (a, b) in enumerate(
+        (
+            (edges_hbm, edges),
+            (weights_hbm, weights),
+            (lengths_hbm, lengths),
+            (counts_hbm, counts),
+            (topo_hbm, topo),
+        )
+    ):
+        copy = pltpu.make_async_copy(a, b, own_sem.at[n])
+        copy.start()
+        small.append(copy)
+    own_leaf = pltpu.make_async_copy(
+        leaf.at[:, :, pl.ds(pl.multiple_of(me * SIDE, SIDE), SIDE)], inbox.at[0], own_sem.at[5]
+    )
+    own_leaf.start()
 
     barrier = pltpu.get_barrier_semaphore()
     for i in range(1, owners):
@@ -184,6 +213,21 @@
         pl.semaphore_signal(
             barrier, inc=1, device_id={"site": lax.rem(my_site + i, site_ways)}, device_id_type=MESH
         )
+
+    meta[...] = jnp.full(meta.shape, -1.0, F32)
+    for copy in small:
+        copy.wait()
+    for level in range(levels):
+        child = edges[level, 0:1, :] - me * node_dev
+        code = edges[level, 2:3, :] * nodes + edges[level, 1:2, :]
+        meta[level, 0:1, 0:edge_dev] = child.astype(F32)
+        meta[level, 1:2, 0:edge_dev] = code.astype(F32)
+        meta[level, 2:3, 0:edge_dev] = weights[level : level + 1, :]
+        meta[level, 3:4, 0:edge_dev] = jnp.exp(lengths[level : level + 1, :] * (-4.0 / 3.0))
+    for t in range(topo_shape[0]):
+        first = edge_dev + t * topo_shape[1]
+        meta[levels - 1, 0:1, first : first + topo_shape[1]] = topo[t : t + 1, :].astype(F32)
+
     pl.semaphore_wait(barrier, owners - 1 + site_ways - 1)
 
     meta_copies, leaf_copies = [], []
@@ -198,8 +242,6 @@
         )
         copy.start()
         meta_copies.append(copy)
-    own_meta = pltpu.make_async_copy(meta, tables.at[0], own_sem.at[0])
-    own_meta.start()
     for i in range(1, owners):
         target = lax.rem(me + i, owners)
         copy = pltpu.make_async_remote_copy(
@@ -212,27 +254,23 @@
         )
         copy.start()
         leaf_copies.append(copy)
-    own_leaf = pltpu.make_async_copy(
-        leaf.at[:, :, pl.ds(pl.multiple_of(me * SIDE, SIDE), SIDE)], inbox.at[0], own_sem.at[1]
-    )
-    own_leaf.start()
-
-    own_meta.wait()
-    for copy in meta_copies:
-        copy.wait_recv()
-
-    def absolute(first, rows):
-        row = lax.broadcasted_iota(jnp.int32, (rows, SIDE), 0) + first
-        node = lax.rem(row, nodes)
-        owner = lax.rem(me - node // node_dev + owners, owners)
-        code = (row // nodes) * nodes + owner * node_dev + lax.rem(node, node_dev)
-        return code.astype(F32)[:, :1]
+    tables[0] = meta[...]
+
+    local = lax.broadcasted_iota(jnp.int32, (node_dev, SIDE), 0)
+    for r in range(2):
+        for i in range(owners):
+            first = r * nodes + i * node_dev
+            owner = lax.rem(me - i + owners, owners)
+            numbers[first : first + node_dev, :] = (
+                local + (r * nodes + owner * node_dev)
+            ).astype(F32)
 
     lane = lax.broadcasted_iota(jnp.int32, (1, SIDE), 1)
     topo_lane = (lane >= SIDE // 2) & (lane < SIDE // 2 + topo_here)
     child_iota = lax.broadcasted_iota(jnp.int32, (2 * node_dev, ROW), 0).astype(F32)
 
-    chunk = 256
+    for copy in meta_copies:
+        copy.wait_recv()
 
     def build(step, carry):
         level = step // (owners // 2)
@@ -250,84 +288,106 @@
             for n, piece in enumerate((g1h, g1l, g2h, g2l)):
                 gmat[n * SIDE : (n + 1) * SIDE, columns] = piece
         code = jnp.concatenate(codes, axis=1)
+
+        def choose(part, inner):
+            rows = pl.ds(pl.multiple_of(part * SIDE, SIDE), SIDE)
+            wide = jnp.concatenate([numbers[rows, :]] * 4, axis=1)
+            picks[duo, rows, :] = jnp.where(wide == code, 1.0, 0.0).astype(BF16)
+            return inner
+
+        lax.fori_loop(0, 2 * nodes // SIDE, choose, 0)
         where_to = pl.ds(pl.multiple_of(duo * SIDE, SIDE), SIDE)
-        for first in range(0, 2 * nodes, chunk):
-            pick = jnp.where(absolute(first, chunk) == code, 1.0, 0.0).astype(BF16)
-            rows = slice(first, first + chunk)
-
-            @pl.when(level == levels - 1)
-            def _():
-                picks[duo, rows, :] = pick
-
-            found = mm_nt(pick, gmat[...])
-            hi, lo = halves(found[:, :SIDE] + found[:, SIDE : 2 * SIDE])
+        for r in range(2):
+            rows = slice(r * nodes, (r + 1) * nodes)
+            found = mm_nt(picks[duo, rows, :], gmat[0 : 2 * SIDE, :])
+            hi, lo = halves(found[:, :SIDE] + found[:, SIDE:])
             m1h[level, rows, where_to] = hi
             m1l[level, rows, where_to] = lo
-            hi, lo = halves(found[:, 2 * SIDE : 3 * SIDE] + found[:, 3 * SIDE :])
+            found = mm_nt(picks[duo, rows, :], gmat[2 * SIDE : 4 * SIDE, :])
+            hi, lo = halves(found[:, :SIDE] + found[:, SIDE:])
             m2h[level, rows, where_to] = hi
             m2l[level, rows, where_to] = lo
         return carry
 
     lax.fori_loop(0, levels * (owners // 2), build, 0)
 
-    node_abs = absolute(0, nodes)
     times = jnp.zeros((nodes, SIDE), F32)
     for i in range(owners):
         wanted = jnp.where(topo_lane, tables[i, levels - 1, 0:1, SIDE:], -1.0)
-        times += jnp.where(node_abs == wanted, 1.0, 0.0)
+        times += jnp.where(numbers[0:nodes, :] == wanted, 1.0, 0.0)
     mult[...] = jnp.broadcast_to(jnp.sum(times, axis=1, keepdims=True), (nodes, SIDE))
 
-    own_leaf.wait()
-    for i in range(owners):
-        if i:
-            leaf_copies[i - 1].wait_recv()
-        block = inbox[i]
-        rows = slice(i * node_dev, (i + 1) * node_dev)
-        for k in range(states):
-            cur[rows, k * SIDE : (k + 1) * SIDE] = block[:, k, :]
-
-    def split(first, carry):
-        rows = pl.ds(pl.multiple_of(first * SIDE, SIDE), SIDE)
-        x = cur[rows, :]
-        chi[rows, :], clo[rows, :] = halves(x)
+    def over_states(x):
         total = x[:, :SIDE]
         for k in range(1, states):
             total = total + x[:, k * SIDE : (k + 1) * SIDE]
-        shi[rows, :], slo[rows, :] = halves(total)
-        return carry
-
-    for level in range(levels):
-        lax.fori_loop(0, nodes // SIDE, split, 0)
-
-        def advance(step, carry, level=level):
+        return total
+
+    def advance(level, slot, first, last, fresh):
+        inner = slice(first, last)
+        for r in range(2):
+            rows = slice(r * nodes, (r + 1) * nodes)
+            bh = m2h[level, rows, inner]
+            flat = mm(bh, sums[slot, inner, :])
+            flat = flat[:, :SIDE] + flat[:, SIDE:]
+            flat = flat + mm(m2l[level, rows, inner], sums[slot, inner, :SIDE])
+            flat = jnp.concatenate([flat, flat], axis=1)
+            for n in range(states // 2):
+                cols = slice(n * ROW, (n + 1) * ROW)
+                full = mm(m1h[level, rows, inner], ch[slot, inner, cols])
+                full = full + mm(m1h[level, rows, inner], cl[slot, inner, cols])
+                full = full + mm(m1l[level, rows, inner], ch[slot, inner, cols])
+                full = full + flat
+                if not fresh:
+                    full = full + pair[rows, cols]
+                pair[rows, cols] = full
+
+    own_leaf.wait()
+    half = owners // 2
+    for part in range(2):
+        for i in range(part * half, (part + 1) * half):
+            if i:
+                leaf_copies[i - 1].wait_recv()
+            block = inbox[i]
+            rows = slice(i * node_dev, (i + 1) * node_dev)
+            total = None
+            for k in range(states):
+                x = block[:, k, :]
+                total = x if k == 0 else total + x
+                cols = slice(k * SIDE, (k + 1) * SIDE)
+                ch[0, rows, cols], cl[0, rows, cols] = halves(x)
+            sums[0, rows, :SIDE], sums[0, rows, SIDE:] = halves(total)
+        advance(0, 0, part * half * node_dev, (part + 1) * half * node_dev, part == 0)
+
+    def multiply(slot):
+        def body(step, carry):
             rows = pl.ds(pl.multiple_of(step * SIDE, SIDE), SIDE)
-            made = []
-            for r in range(2):
-                source = pl.ds(pl.multiple_of(r * nodes + step * SIDE, SIDE), SIDE)
-                ah, al = m1h[level, source, :], m1l[level, source, :]
-                bh, bl = m2h[level, source, :], m2l[level, source, :]
-                flat = mm(bh, shi[...]) + mm(bh, slo[...]) + mm(bl, shi[...])
-                full = mm(ah, chi[...]) + mm(ah, clo[...]) + mm(al, chi[...])
-                made.append(full + jnp.concatenate([flat] * states, axis=1))
-                if level == levels - 1:
-                    pair[source, :] = made[r]
-            cur[rows, :] = made[0] * made[1]
+            other = pl.ds(pl.multiple_of(nodes + step * SIDE, SIDE), SIDE)
+            x = pair[rows, :] * pair[other, :]
+            ch[slot, rows, :], cl[slot, rows, :] = halves(x)
+            sums[slot, rows, :SIDE], sums[slot, rows, SIDE:] = halves(over_states(x))
             return carry
 
-        lax.fori_loop(0, nodes // SIDE, advance, 0)
-
-    site_row = lax.broadcasted_iota(jnp.int32, scaled.shape, 0)
-    count = jnp.sum(jnp.where(site_row == me, scaled[...], 0.0), axis=0, keepdims=True)
+        lax.fori_loop(0, nodes // SIDE, body, 0)
+
+    slot = 0
+    for level in range(1, levels):
+        slot = level % 2
+        multiply(slot)
+        advance(level, slot, 0, nodes, True)
+
+    site_row = lax.broadcasted_iota(jnp.int32, counts.shape, 0)
+    count = jnp.sum(
+        jnp.where(site_row == me, counts[...].astype(F32) / sites_all, 0.0), axis=0, keepdims=True
+    )
     picked = [jnp.zeros((1, SIDE), F32)] * owners
     for first in range(0, nodes, SIDE):
         rows = slice(first, first + SIDE)
-        x = cur[rows, :]
-        total = x[:, :SIDE]
-        for k in range(1, states):
-            total = total + x[:, k * SIDE : (k + 1) * SIDE]
-        lik = 0.25 * total
+        p0 = pair[rows, :]
+        p1 = pair[nodes + first : nodes + first + SIDE, :]
+        lik = 0.25 * over_states(p0 * p1)
         score = jnp.sum(count * jnp.log(lik), axis=1, keepdims=True)
-        here = absolute(first, SIDE)
+        here = numbers[rows, :]
         for i in range(owners):
             wanted = jnp.where(topo_lane, tables[i, levels - 1, 0:1, SIDE:], -1.0)
             picked[i] = picked[i] + jnp.sum(
@@ -336,20 +396,18 @@
         factor = count * 0.25 / lik * mult[rows, :]
         wide = jnp.concatenate([factor] * states, axis=1)
         for r in range(2):
-            adj = pair[(1 - r) * nodes + first : (1 - r) * nodes + first + SIDE, :] * wide
+            adj = (p0 if r else p1) * wide
             to = slice(r * nodes + first, r * nodes + first + SIDE)
             ahi[to, :], alo[to, :] = halves(adj)
-            flat = adj[:, :SIDE]
-            for k in range(1, states):
-                flat = flat + adj[:, k * SIDE : (k + 1) * SIDE]
-            shadj_hi[to, :], shadj_lo[to, :] = halves(flat)
+            adj_sums[to, :SIDE], adj_sums[to, SIDE:] = halves(over_states(adj))
 
     def products(step, carry):
         cols = pl.ds(pl.multiple_of(step * ROW, ROW), ROW)
         ah, al = ahi[cols, :], alo[cols, :]
-        sh, sl = shadj_hi[cols, :], shadj_lo[cols, :]
-        d1 = mm_nt(chi[...], ah) + mm_nt(chi[...], al) + mm_nt(clo[...], ah)
-        d2 = mm_nt(shi[...], sh) + mm_nt(shi[...], sl) + mm_nt(slo[...], sh)
+        both = adj_sums[cols, :]
+        d1 = mm_nt(ch[slot], ah) + mm_nt(ch[slot], al) + mm_nt(cl[slot], ah)
+        turned = jnp.concatenate([both[:, SIDE:], both[:, :SIDE]], axis=1)
+        d2 = mm_nt(sums[slot], both) + mm_nt(sums[slot], turned)
         d1h, d1l = halves(d1)
         d2h, d2l = halves(d2)
         for i in range(owners):
@@ -362,7 +420,9 @@
 
     edge_iota = lax.broadcasted_iota(jnp.int32, (node_dev, ROW), 0).astype(F32)
     last = levels - 1
-    for i in range(owners):
+    first_copies = []
+    for step in range(owners):
+        i = (step + 1) % owners
         found = mm(dst[i], picks[i // 2, :, (i % 2) * ROW : (i % 2 + 1) * ROW])
         hot = edge_iota == tables[i, last, 0:1, :]
         d1 = found[:node_dev] + found[node_dev : 2 * node_dev]
@@ -372,9 +432,8 @@
         grads = jnp.sum(mixed, axis=0, keepdims=True)
         grads = grads + jnp.concatenate([jnp.zeros((1, SIDE), F32), picked[i]], axis=1)
         send1[i] = jnp.broadcast_to(grads, (8, ROW))
-
-    first_copies = []
-    for i in range(1, owners):
+        if i == 0:
+            continue
         copy = pltpu.make_async_remote_copy(
             src_ref=send1.at[i],
             dst_ref=recv1.at[i],
@@ -403,13 +462,23 @@
         )
         copy.start()
         second_copies.append(copy)
+    for copy in meta_copies + leaf_copies + first_copies:
+        copy.wait_send()
     for copy in second_copies:
         copy.wait_recv()
     total = recv2[0]
     for i in range(1, site_ways):
         total = total + recv2[i]
-    out[...] = total
-    for copy in meta_copies + leaf_copies + first_copies + second_copies:
+    grad_out[...] = total[0, 0:edge_dev]
+    tail = total[0:1, SIDE:]
+    which = (lane - SIDE // 2) // topo_shape[1]
+    here = jnp.zeros((1, SIDE), F32)
+    for t in range(topo_shape[0]):
+        mine = topo_lane & (which == t)
+        score = jnp.sum(jnp.where(mine, tail, 0.0), axis=1, keepdims=True)
+        here = here + jnp.where(lane == t, score, 0.0)
+    loglik_out[...] = here[0, 0 : topo_shape[0]]
+    for copy in second_copies:
         copy.wait_send()
 
 
@@ -418,56 +487,54 @@
     levels, edge_dev, _ = dag_edges.shape
     owners, site_ways = lax.axis_size("node"), lax.axis_size("site")
     nodes = owners * node_dev
-    topo_here = topo_nodes.size
-    edges = jnp.transpose(dag_edges, (2, 0, 1))
-    child = edges[0] - lax.axis_index("node") * node_dev
-    code = edges[2] * nodes + edges[1]
-    tail = ROW - edge_dev
-    extra = jnp.pad(topo_nodes.reshape(-1), (0, tail - topo_here))
-    child = jnp.concatenate([child, jnp.broadcast_to(extra, (levels, tail))], axis=1)
-    pad = ((0, 0), (0, tail))
-    meta = jnp.stack(
-        [
-            child.astype(F32),
-            jnp.pad(code, pad, constant_values=-1).astype(F32),
-            jnp.pad(weights, pad),
-            jnp.pad(jnp.exp(lengths * (-4.0 / 3.0)), pad),
-        ],
-        axis=1,
-    )
-    scaled = (counts.astype(F32) / (site_dev * site_ways)).reshape(owners, SIDE)
     wide = states * SIDE
-    out = pl.pallas_call(
+    far = pl.BlockSpec(memory_space=pltpu.HBM)
+    near = pl.BlockSpec(memory_space=pltpu.VMEM)
+    operator = pltpu.VMEM((levels, 2 * nodes, nodes), BF16)
+    loglik, grads = pl.pallas_call(
         functools.partial(
-            kernel, (owners, site_ways, node_dev, states, levels, topo_here)
+            kernel,
+            (
+                owners,
+                site_ways,
+                node_dev,
+                states,
+                levels,
+                topo_nodes.shape,
+                site_dev * site_ways,
+            ),
         ),
-        out_shape=jax.ShapeDtypeStruct((8, ROW), F32),
-        in_specs=[
-            pl.BlockSpec(memory_space=pl.ANY),
-            pl.BlockSpec(memory_space=pltpu.VMEM),
-            pl.BlockSpec(memory_space=pltpu.VMEM),
-        ],
-        out_specs=pl.BlockSpec(memory_space=pltpu.VMEM),
+        out_shape=(
+            jax.ShapeDtypeStruct((topo_nodes.shape[0],), F32),
+            jax.ShapeDtypeStruct((edge_dev,), F32),
+        ),
+        in_specs=[far] * 6,
+        out_specs=(near, near),
         scratch_shapes=[
+            pltpu.VMEM((levels, 3, edge_dev), jnp.int32),
+            pltpu.VMEM((levels, edge_dev), F32),
+            pltpu.VMEM((levels, edge_dev), F32),
+            pltpu.VMEM((owners, SIDE), jnp.int32),
+            pltpu.VMEM(topo_nodes.shape, jnp.int32),
+            pltpu.VMEM((levels, 4, ROW), F32),
             pltpu.VMEM((owners, node_dev, states, SIDE), F32),
             pltpu.VMEM((owners, levels, 4, ROW), F32),
-            pltpu.VMEM((levels, 2 * nodes, nodes), BF16),
-            pltpu.VMEM((levels, 2 * nodes, nodes), BF16),
-            pltpu.VMEM((levels, 2 * nodes, nodes), BF16),
-            pltpu.VMEM((levels, 2 * nodes, nodes), BF16),
+            operator,
+            operator,
+            operator,
+            operator,
             pltpu.VMEM((owners // 2, 2 * nodes, 2 * ROW), BF16),
             pltpu.VMEM((4 * SIDE, 2 * ROW), BF16),
-            pltpu.VMEM((nodes, wide), BF16),
-            pltpu.VMEM((nodes, wide), BF16),
-            pltpu.VMEM((nodes, SIDE), BF16),
-            pltpu.VMEM((nodes, SIDE), BF16),
-            pltpu.VMEM((nodes, wide), F32),
+            pltpu.VMEM((2, nodes, wide), BF16),
+            pltpu.VMEM((2, nodes, wide), BF16),
+            pltpu.VMEM((2, nodes, 2 * SIDE), BF16),
             pltpu.VMEM((2 * nodes, wide), F32),
+            pltpu.VMEM((nodes, SIDE), F32),
             pltpu.VMEM((2 * nodes, wide), BF16),
             pltpu.VMEM((2 * nodes, wide), BF16),
-            pltpu.VMEM((2 * nodes, SIDE), BF16),
-            pltpu.VMEM((2 * nodes, SIDE), BF16),
+            pltpu.VMEM((2 * nodes, 2 * SIDE), BF16),
             pltpu.VMEM((owners, 4 * node_dev, 2 * nodes), BF16),
+            pltpu.VMEM((2 * nodes, SIDE), F32),
             pltpu.VMEM((nodes, SIDE), F32),
             pltpu.VMEM((owners, 8, ROW), F32),
             pltpu.VMEM((owners, 8, ROW), F32),
@@ -477,20 +544,24 @@
             pltpu.SemaphoreType.DMA((owners,)),
             pltpu.SemaphoreType.DMA((owners,)),
             pltpu.SemaphoreType.DMA((owners,)),
-            pltpu.SemaphoreType.DMA((2,)),
+            pltpu.SemaphoreType.DMA((6,)),
             pltpu.SemaphoreType.DMA((owners,)),
             pltpu.SemaphoreType.DMA((owners,)),
             pltpu.SemaphoreType.DMA((site_ways,)),
             pltpu.SemaphoreType.DMA((site_ways,)),
         ],
         compiler_params=pltpu.CompilerParams(
-            collective_id=0, has_side_effects=True, vmem_limit_bytes=50 * 2**20
+            collective_id=0, has_side_effects=True, vmem_limit_bytes=64 * 2**20
         ),
-    )(leaf_partials, meta, scaled)
-    loglik = jnp.sum(
-        out[0, edge_dev : edge_dev + topo_here].reshape(topo_nodes.shape), axis=1
-    )
-    return loglik, out[0, :edge_dev]
+    )(
+        leaf_partials,
+        jnp.transpose(dag_edges, (0, 2, 1)),
+        weights,
+        lengths,
+        counts.reshape(owners, SIDE),
+        topo_nodes,
+    )
+    return loglik, grads
 
 
 def either(leaf_partials, dag_edges, weights, lengths, counts, topo_nodes):

time: 73.7 us -> 58.6 us (0.80)
  Pallas kernels: 66.5 us -> 55.8 us
  local copies, waits for them, and re-layouts: 5.53 us -> 1.86 us
    pallas_call x1, Pallas kernels: 66.5 us -> 55.8 us  [by_sites(): pl.pallas_call(functools.partial(kernel, (owners, site_ways, node_dev, st...]
    unnamed x11 -> x6, local copies, waits for them, and re-layouts: 4.61 us -> 1.86 us
where the time goes in v2:
time: 58.6 us; the launch traced here: 58.3 us
  Pallas kernels  55.8 us (95%)
  local copies, waits for them, and re-layouts  1.86 us (3%)
  between operations  0.65 us (1%)
    pallas_call x1, Pallas kernels, by_sites(): pl.pallas_call(functools.partial(kernel, (owners, site_ways, node_dev, st...  55.8 us
    unnamed x6, local copies, waits for them, and re-layouts  1.86 us

profile of v2, /device:TPU:0, one launch (start us, length us, event | category | flops | bytes accessed | tf_op | source)
XLA Modules:
  0.0 58.3 jit_solution(15259388874080676679)
XLA Ops:
  0.6 55.8 %shard_map.77 = (f32[4]{0:T(128)}, f32[192]{0:T(256)}) custom-call(f32[64,4,1024]{2,1,0:T(4,128)} %leaf.1, s32[3,3,192]{2,1,0:T(4,128)} %bitcast.2, f32[3,192]{1,0:T(4,128)} %weights_hbm.1, f32[3,192]{1,0:T(4,128)} %lengths_hbm.1, s32[8,128]{1,0:T(8,128)} %bitcast.3, s32[4,8]{1,0:T(4,128)} %topo_hbm.1), custom_call_target="tpu_custom_call" | custom-call | tf_op jit(solution)/shard_map/pallas_call | solution.py:494
  56.5 0.0 copy-start.1
  56.5 0.6 %copy-done.1 = f32[4]{0:T(128)S(1)} copy-done((f32[4]{0:T(128)S(1)}, f32[4]{0:T(128)}, u32[]{:S(2)}) %copy-start.1) | copy-done | bytes 40
  57.1 0.0 copy-start
  57.1 0.5 copy.10
  57.6 0.2 copy-done
  57.8 0.6 copy.11
Async XLA Ops:
  56.5 0.6 %copy-start.1 = (f32[4]{0:T(128)S(1)}, f32[4]{0:T(128)}, u32[]{:S(2)}) copy-start(f32[4]{0:T(128)} %get-tuple-element.4) | copy-start | bytes 52
  57.1 0.7 %copy-start = (f32[192]{0:T(256)S(1)}, f32[192]{0:T(256)}, u32[]{:S(2)}) copy-start(f32[192]{0:T(256)} %get-tuple-element.5) | copy-start | bytes 2308

commit v3 on v2

--- a/solution.py
+++ b/solution.py
@@ -148,20 +148,14 @@
     meta,
     inbox,
     tables,
-    m1h,
-    m1l,
+    m1,
     m2h,
     m2l,
     picks,
     gmat,
-    ch,
-    cl,
+    stack,
     sums,
     pair,
-    lik_sum,
-    ahi,
-    alo,
-    adj_sums,
     dst,
     numbers,
     mult,
@@ -272,6 +266,8 @@
     for copy in meta_copies:
         copy.wait_recv()
 
+    half = nodes // 2
+
     def build(step, carry):
         level = step // (owners // 2)
         duo = lax.rem(step, owners // 2)
@@ -297,16 +293,19 @@
 
         lax.fori_loop(0, 2 * nodes // SIDE, choose, 0)
         where_to = pl.ds(pl.multiple_of(duo * SIDE, SIDE), SIDE)
+        base = (duo // (owners // 4)) * 3 * half + lax.rem(duo, owners // 4) * SIDE
+        thirds = [pl.ds(pl.multiple_of(base + n * half, SIDE), SIDE) for n in range(3)]
         for r in range(2):
             rows = slice(r * nodes, (r + 1) * nodes)
             found = mm_nt(picks[duo, rows, :], gmat[0 : 2 * SIDE, :])
             hi, lo = halves(found[:, :SIDE] + found[:, SIDE:])
-            m1h[level, rows, where_to] = hi
-            m1l[level, rows, where_to] = lo
+            m1[level, r, :, thirds[0]] = hi
+            m1[level, r, :, thirds[1]] = hi
+            m1[level, r, :, thirds[2]] = lo
             found = mm_nt(picks[duo, rows, :], gmat[2 * SIDE : 4 * SIDE, :])
             hi, lo = halves(found[:, :SIDE] + found[:, SIDE:])
-            m2h[level, rows, where_to] = hi
-            m2l[level, rows, where_to] = lo
+            m2h[level, r, :, where_to] = hi
+            m2l[level, r, :, where_to] = lo
         return carry
 
     lax.fori_loop(0, levels * (owners // 2), build, 0)
@@ -323,100 +322,114 @@
             total = total + x[:, k * SIDE : (k + 1) * SIDE]
         return total
 
-    def advance(level, slot, first, last, fresh):
-        inner = slice(first, last)
-        for r in range(2):
-            rows = slice(r * nodes, (r + 1) * nodes)
-            bh = m2h[level, rows, inner]
-            flat = mm(bh, sums[slot, inner, :])
-            flat = flat[:, :SIDE] + flat[:, SIDE:]
-            flat = flat + mm(m2l[level, rows, inner], sums[slot, inner, :SIDE])
+    def keep(slot, g, cols, x):
+        base = g * 3 * half
+        hi, lo = halves(x)
+        for n, piece in enumerate((hi, lo, hi)):
+            rows = pl.ds(pl.multiple_of(base + n * half, half), half)
+            stack[slot, rows, cols] = piece
+
+    def advance(level, slot, parts, fresh, store, later):
+        inner = slice(parts[0] * half, parts[1] * half)
+        long = slice(parts[0] * 3 * half, parts[1] * 3 * half)
+
+        def body(g, carry):
+            rows = pl.ds(pl.multiple_of(g * half, half), half)
+            high = m2h[level, :, rows, inner].reshape(2 * half, -1)
+            low = m2l[level, :, rows, inner].reshape(2 * half, -1)
+            flat = mm(high, sums[slot, inner, :])
+            flat = flat[:, :SIDE] + flat[:, SIDE:] + mm(low, sums[slot, inner, :SIDE])
             flat = jnp.concatenate([flat, flat], axis=1)
+            left = m1[level, :, rows, long].reshape(2 * half, -1)
+            total = None
             for n in range(states // 2):
                 cols = slice(n * ROW, (n + 1) * ROW)
-                full = mm(m1h[level, rows, inner], ch[slot, inner, cols])
-                full = full + mm(m1h[level, rows, inner], cl[slot, inner, cols])
-                full = full + mm(m1l[level, rows, inner], ch[slot, inner, cols])
-                full = full + flat
+                full = mm(left, stack[slot, long, cols]) + flat
                 if not fresh:
-                    full = full + pair[rows, cols]
-                pair[rows, cols] = full
+                    full = full + pair[:, rows, cols].reshape(2 * half, ROW)
+                if store:
+                    pair[:, rows, cols] = full.reshape(2, half, ROW)
+                if later is not None:
+                    x = full[:half] * full[half:]
+                    keep(later, g, cols, x)
+                    x = x[:, :SIDE] + x[:, SIDE:]
+                    total = x if n == 0 else total + x
+            if later is not None:
+                sums[later, rows, :SIDE], sums[later, rows, SIDE:] = halves(total)
+            return carry
+
+        lax.fori_loop(0, 2, body, 0)
 
     own_leaf.wait()
-    half = owners // 2
     for part in range(2):
-        for i in range(part * half, (part + 1) * half):
+        for i in range(part * owners // 2, (part + 1) * owners // 2):
             if i:
                 leaf_copies[i - 1].wait_recv()
             block = inbox[i]
             rows = slice(i * node_dev, (i + 1) * node_dev)
+            base = part * 3 * half + i * node_dev - part * half
             total = None
             for k in range(states):
                 x = block[:, k, :]
                 total = x if k == 0 else total + x
-                cols = slice(k * SIDE, (k + 1) * SIDE)
-                ch[0, rows, cols], cl[0, rows, cols] = halves(x)
+                hi, lo = halves(x)
+                for n, piece in enumerate((hi, lo, hi)):
+                    to = slice(base + n * half, base + n * half + node_dev)
+                    stack[0, to, k * SIDE : (k + 1) * SIDE] = piece
             sums[0, rows, :SIDE], sums[0, rows, SIDE:] = halves(total)
-        advance(0, 0, part * half * node_dev, (part + 1) * half * node_dev, part == 0)
-
-    def multiply(slot):
-        def body(step, carry):
-            rows = pl.ds(pl.multiple_of(step * SIDE, SIDE), SIDE)
-            other = pl.ds(pl.multiple_of(nodes + step * SIDE, SIDE), SIDE)
-            x = pair[rows, :] * pair[other, :]
-            ch[slot, rows, :], cl[slot, rows, :] = halves(x)
-            sums[slot, rows, :SIDE], sums[slot, rows, SIDE:] = halves(over_states(x))
-            return carry
-
-        lax.fori_loop(0, nodes // SIDE, body, 0)
-
-    slot = 0
+        advance(0, 0, (part, part + 1), part == 0, part == 0, 1 if part else None)
     for level in range(1, levels):
-        slot = level % 2
-        multiply(slot)
-        advance(level, slot, 0, nodes, True)
+        last_one = level == levels - 1
+        advance(level, level % 2, (0, 2), True, last_one, None if last_one else (level + 1) % 2)
+    slot = (levels - 1) % 2
 
     site_row = lax.broadcasted_iota(jnp.int32, counts.shape, 0)
     count = jnp.sum(
         jnp.where(site_row == me, counts[...].astype(F32) / sites_all, 0.0), axis=0, keepdims=True
     )
-    picked = [jnp.zeros((1, SIDE), F32)] * owners
-    for first in range(0, nodes, SIDE):
-        rows = slice(first, first + SIDE)
-        p0 = pair[rows, :]
-        p1 = pair[nodes + first : nodes + first + SIDE, :]
+
+    def products(step, picked):
+        rows = pl.ds(pl.multiple_of(step * SIDE, SIDE), SIDE)
+        p0 = pair[0, rows, :]
+        p1 = pair[1, rows, :]
         lik = 0.25 * over_states(p0 * p1)
+        factor = count * 0.25 / lik * mult[rows, :]
+        wide = jnp.concatenate([factor] * states, axis=1)
+        adj = jnp.concatenate([p1 * wide, p0 * wide], axis=0)
+        ah, al = halves(adj)
+        sh, sl = halves(over_states(adj))
+        both = jnp.concatenate([sh, sl], axis=1)
+        turned = jnp.concatenate([sl, sh], axis=1)
+        for part in range(2):
+            base = part * 3 * half
+            d1 = mm_nt(stack[slot, base : base + 2 * half, :], ah)
+            d1 = d1[:half] + d1[half:] + mm_nt(stack[slot, base : base + half, :], al)
+            own = sums[slot, part * half : (part + 1) * half, :]
+            d2 = mm_nt(own, both) + mm_nt(own, turned)
+            pieces = halves(d1) + halves(d2)
+            for i in range(owners // 2):
+                inner = slice(i * node_dev, (i + 1) * node_dev)
+                for n, piece in enumerate(pieces):
+                    to = slice(n * node_dev, (n + 1) * node_dev)
+                    for r in range(2):
+                        cols = pl.ds(pl.multiple_of(r * nodes + step * SIDE, SIDE), SIDE)
+                        dst[part * owners // 2 + i, to, cols] = piece[
+                            inner, r * SIDE : (r + 1) * SIDE
+                        ]
         score = jnp.sum(count * jnp.log(lik), axis=1, keepdims=True)
         here = numbers[rows, :]
+        found = []
         for i in range(owners):
             wanted = jnp.where(topo_lane, tables[i, levels - 1, 0:1, SIDE:], -1.0)
-            picked[i] = picked[i] + jnp.sum(
-                jnp.where(here == wanted, score, 0.0), axis=0, keepdims=True
+            found.append(
+                picked[i]
+                + jnp.sum(jnp.where(here == wanted, score, 0.0), axis=0, keepdims=True)
             )
-        factor = count * 0.25 / lik * mult[rows, :]
-        wide = jnp.concatenate([factor] * states, axis=1)
-        for r in range(2):
-            adj = (p0 if r else p1) * wide
-            to = slice(r * nodes + first, r * nodes + first + SIDE)
-            ahi[to, :], alo[to, :] = halves(adj)
-            adj_sums[to, :SIDE], adj_sums[to, SIDE:] = halves(over_states(adj))
-
-    def products(step, carry):
-        cols = pl.ds(pl.multiple_of(step * ROW, ROW), ROW)
-        ah, al = ahi[cols, :], alo[cols, :]
-        both = adj_sums[cols, :]
-        d1 = mm_nt(ch[slot], ah) + mm_nt(ch[slot], al) + mm_nt(cl[slot], ah)
-        turned = jnp.concatenate([both[:, SIDE:], both[:, :SIDE]], axis=1)
-        d2 = mm_nt(sums[slot], both) + mm_nt(sums[slot], turned)
-        d1h, d1l = halves(d1)
-        d2h, d2l = halves(d2)
-        for i in range(owners):
-            rows = slice(i * node_dev, (i + 1) * node_dev)
-            for n, piece in enumerate((d1h, d1l, d2h, d2l)):
-                dst[i, n * node_dev : (n + 1) * node_dev, cols] = piece[rows, :]
-        return carry
-
-    lax.fori_loop(0, 2 * nodes // ROW, products, 0)
+        return tuple(found)
+
+    picked = lax.fori_loop(
+        0, nodes // SIDE, products, tuple(jnp.zeros((1, SIDE), F32) for _ in range(owners))
+    )
 
     edge_iota = lax.broadcasted_iota(jnp.int32, (node_dev, ROW), 0).astype(F32)
     last = levels - 1
@@ -490,7 +503,7 @@
     wide = states * SIDE
     far = pl.BlockSpec(memory_space=pltpu.HBM)
     near = pl.BlockSpec(memory_space=pltpu.VMEM)
-    operator = pltpu.VMEM((levels, 2 * nodes, nodes), BF16)
+    operator = pltpu.VMEM((levels, 2, nodes, nodes), BF16)
     loglik, grads = pl.pallas_call(
         functools.partial(
             kernel,
@@ -519,20 +532,14 @@
             pltpu.VMEM((levels, 4, ROW), F32),
             pltpu.VMEM((owners, node_dev, states, SIDE), F32),
             pltpu.VMEM((owners, levels, 4, ROW), F32),
-            operator,
-            operator,
+            pltpu.VMEM((levels, 2, nodes, 3 * nodes), BF16),
             operator,
             operator,
             pltpu.VMEM((owners // 2, 2 * nodes, 2 * ROW), BF16),
             pltpu.VMEM((4 * SIDE, 2 * ROW), BF16),
-            pltpu.VMEM((2, nodes, wide), BF16),
-            pltpu.VMEM((2, nodes, wide), BF16),
+            pltpu.VMEM((2, 3 * nodes, wide), BF16),
             pltpu.VMEM((2, nodes, 2 * SIDE), BF16),
-            pltpu.VMEM((2 * nodes, wide), F32),
-            pltpu.VMEM((nodes, SIDE), F32),
-            pltpu.VMEM((2 * nodes, wide), BF16),
-            pltpu.VMEM((2 * nodes, wide), BF16),
-            pltpu.VMEM((2 * nodes, 2 * SIDE), BF16),
+            pltpu.VMEM((2, nodes, wide), F32),
             pltpu.VMEM((owners, 4 * node_dev, 2 * nodes), BF16),
             pltpu.VMEM((2 * nodes, SIDE), F32),
             pltpu.VMEM((nodes, SIDE), F32),
@@ -570,7 +577,7 @@
     fits = (
         site_dev == owners * SIDE
         and 2 * node_dev == SIDE
-        and owners % 2 == 0
+        and owners % 4 == 0
         and owners <= 8
         and dag_edges.shape[1] == ROW * 3 // 4
         and topo_nodes.size <= ROW // 4

time: 58.6 us -> 62.8 us (1.072)
  Pallas kernels: 55.8 us -> 60.1 us
    pallas_call x1, Pallas kernels: 55.8 us -> 60.1 us  [by_sites(): pl.pallas_call(functools.partial(kernel, (owners, site_ways, node_dev, st...]
where the time goes in v3:
time: 62.8 us; the launch traced here: 62.6 us
  Pallas kernels  60.1 us (96%)
  local copies, waits for them, and re-layouts  1.86 us (3%)
  between operations  0.65 us (1%)
    pallas_call x1, Pallas kernels, by_sites(): pl.pallas_call(functools.partial(kernel, (owners, site_ways, node_dev, st...  60.1 us
    unnamed x6, local copies, waits for them, and re-layouts  1.86 us

profile of v3, /device:TPU:0, one launch (start us, length us, event | category | flops | bytes accessed | tf_op | source)
XLA Modules:
  0.0 62.6 jit_solution(3138414695909564659)
XLA Ops:
  0.6 60.1 %shard_map.77 = (f32[4]{0:T(128)}, f32[192]{0:T(256)}) custom-call(f32[64,4,1024]{2,1,0:T(4,128)} %leaf.1, s32[3,3,192]{2,1,0:T(4,128)} %bitcast.2, f32[3,192]{1,0:T(4,128)} %weights_hbm.1, f32[3,192]{1,0:T(4,128)} %lengths_hbm.1, s32[8,128]{1,0:T(8,128)} %bitcast.3, s32[4,8]{1,0:T(4,128)} %topo_hbm.1), custom_call_target="tpu_custom_call" | custom-call | tf_op jit(solution)/shard_map/pallas_call | solution.py:507
  60.7 0.0 copy-start.1
  60.7 0.6 copy-done.1
  61.3 0.0 copy-start
  61.4 0.5 copy.10
  61.9 0.2 copy-done
  62.0 0.6 copy.11
Async XLA Ops:
  60.7 0.6 %copy-start.1 = (f32[4]{0:T(128)S(1)}, f32[4]{0:T(128)}, u32[]{:S(2)}) copy-start(f32[4]{0:T(128)} %get-tuple-element.4) | copy-start | bytes 52
  61.3 0.7 %copy-start = (f32[192]{0:T(256)S(1)}, f32[192]{0:T(256)}, u32[]{:S(2)}) copy-start(f32[192]{0:T(256)} %get-tuple-element.5) | copy-start | bytes 2308

commit v4 on v2

--- a/solution.py
+++ b/solution.py
@@ -289,13 +289,10 @@
                 gmat[n * SIDE : (n + 1) * SIDE, columns] = piece
         code = jnp.concatenate(codes, axis=1)
 
-        def choose(part, inner):
-            rows = pl.ds(pl.multiple_of(part * SIDE, SIDE), SIDE)
+        for part in range(2 * nodes // SIDE):
+            rows = slice(part * SIDE, (part + 1) * SIDE)
             wide = jnp.concatenate([numbers[rows, :]] * 4, axis=1)
             picks[duo, rows, :] = jnp.where(wide == code, 1.0, 0.0).astype(BF16)
-            return inner
-
-        lax.fori_loop(0, 2 * nodes // SIDE, choose, 0)
         where_to = pl.ds(pl.multiple_of(duo * SIDE, SIDE), SIDE)
         for r in range(2):
             rows = slice(r * nodes, (r + 1) * nodes)
@@ -360,15 +357,12 @@
         advance(0, 0, part * half * node_dev, (part + 1) * half * node_dev, part == 0)
 
     def multiply(slot):
-        def body(step, carry):
-            rows = pl.ds(pl.multiple_of(step * SIDE, SIDE), SIDE)
-            other = pl.ds(pl.multiple_of(nodes + step * SIDE, SIDE), SIDE)
+        for step in range(nodes // SIDE):
+            rows = slice(step * SIDE, (step + 1) * SIDE)
+            other = slice(nodes + step * SIDE, nodes + (step + 1) * SIDE)
             x = pair[rows, :] * pair[other, :]
             ch[slot, rows, :], cl[slot, rows, :] = halves(x)
             sums[slot, rows, :SIDE], sums[slot, rows, SIDE:] = halves(over_states(x))
-            return carry
-
-        lax.fori_loop(0, nodes // SIDE, body, 0)
 
     slot = 0
     for level in range(1, levels):
@@ -401,8 +395,8 @@
             ahi[to, :], alo[to, :] = halves(adj)
             adj_sums[to, :SIDE], adj_sums[to, SIDE:] = halves(over_states(adj))
 
-    def products(step, carry):
-        cols = pl.ds(pl.multiple_of(step * ROW, ROW), ROW)
+    for step in range(2 * nodes // ROW):
+        cols = slice(step * ROW, (step + 1) * ROW)
         ah, al = ahi[cols, :], alo[cols, :]
         both = adj_sums[cols, :]
         d1 = mm_nt(ch[slot], ah) + mm_nt(ch[slot], al) + mm_nt(cl[slot], ah)
@@ -414,9 +408,6 @@
             rows = slice(i * node_dev, (i + 1) * node_dev)
             for n, piece in enumerate((d1h, d1l, d2h, d2l)):
                 dst[i, n * node_dev : (n + 1) * node_dev, cols] = piece[rows, :]
-        return carry
-
-    lax.fori_loop(0, 2 * nodes // ROW, products, 0)
 
     edge_iota = lax.broadcasted_iota(jnp.int32, (node_dev, ROW), 0).astype(F32)
     last = levels - 1

time: 58.6 us -> 55.8 us (0.952)
  Pallas kernels: 55.8 us -> 53.1 us
    pallas_call x1, Pallas kernels: 55.8 us -> 53.1 us  [by_sites(): pl.pallas_call(functools.partial(kernel, (owners, site_ways, node_dev, st...]
where the time goes in v4:
time: 55.8 us; the launch traced here: 55.6 us
  Pallas kernels  53.1 us (95%)
  local copies, waits for them, and re-layouts  1.86 us (3%)
  between operations  0.65 us (1%)
    pallas_call x1, Pallas kernels, by_sites(): pl.pallas_call(functools.partial(kernel, (owners, site_ways, node_dev, st...  53.1 us
    unnamed x6, local copies, waits for them, and re-layouts  1.86 us

profile of v4, /device:TPU:0, one launch (start us, length us, event | category | flops | bytes accessed | tf_op | source)
XLA Modules:
  0.0 55.6 jit_solution(11310658036440377460)
XLA Ops:
  0.6 53.1 %shard_map.77 = (f32[4]{0:T(128)}, f32[192]{0:T(256)}) custom-call(f32[64,4,1024]{2,1,0:T(4,128)} %leaf.1, s32[3,3,192]{2,1,0:T(4,128)} %bitcast.2, f32[3,192]{1,0:T(4,128)} %weights_hbm.1, f32[3,192]{1,0:T(4,128)} %lengths_hbm.1, s32[8,128]{1,0:T(8,128)} %bitcast.3, s32[4,8]{1,0:T(4,128)} %topo_hbm.1), custom_call_target="tpu_custom_call" | custom-call | tf_op jit(solution)/shard_map/pallas_call | solution.py:485
  53.7 0.0 copy-start.1
  53.7 0.6 %copy-done.1 = f32[4]{0:T(128)S(1)} copy-done((f32[4]{0:T(128)S(1)}, f32[4]{0:T(128)}, u32[]{:S(2)}) %copy-start.1) | copy-done | bytes 40
  54.3 0.0 copy-start
  54.3 0.5 copy.10
  54.9 0.2 copy-done
  55.0 0.6 %copy.11 = f32[192]{0:T(256)} copy(f32[192]{0:T(256)S(1)} %copy-done) | data formatting | bytes 1536
Async XLA Ops:
  53.7 0.6 %copy-start.1 = (f32[4]{0:T(128)S(1)}, f32[4]{0:T(128)}, u32[]{:S(2)}) copy-start(f32[4]{0:T(128)} %get-tuple-element.4) | copy-start | bytes 52
  54.3 0.7 %copy-start = (f32[192]{0:T(256)S(1)}, f32[192]{0:T(256)}, u32[]{:S(2)}) copy-start(f32[192]{0:T(256)} %get-tuple-element.5) | copy-start | bytes 2308
